TPU v7x, 32 devices: a whole 2x2x4 slice. The times are simulated.
32 devices in a mesh: region: 4 (over x, core), dev: 8 (over z, y).
Axes of the slice: x: 2, y: 2, z: 4, core: 2. Of those that a mesh axis runs over, the one named last changes fastest.
Arguments:
- synthetic: bfloat16 [512, 3, 4096], P(('region', 'dev')), may hold values from -6 to 6
- observed: bfloat16 [512, 3, 4096], P(('region', 'dev')), may hold values from -6 to 6
- nearby_receiver_slots: int32 [256, 4], P(('region', 'dev')), may hold values from 0 to 15
- far_rows: int32 [256, 4], P(('region', 'dev')), may hold values from 0 to 15
- first_slot: int32 [8192], P(('region', 'dev')), may hold values from 0 to 31
- second_slot: int32 [8192], P(('region', 'dev')), may hold values from 0 to 63
- window_start: int32 [8192], P(('region', 'dev')), may hold values from 0 to 255
- pair_delay_indices: int32 [8192], P(('region', 'dev')), may hold values from 64 to 256
Outputs:
- adjoint: bfloat16 [512, 3, 4096], P(('region', 'dev'))
- misfit: float32 [8192], P(('region', 'dev'))
All inputs are finite; a program needn't handle non-finite values.
Results may differ from a plain program's by a relative error of at most 0.0084.
Values may be sent and summed in bfloat16 or wider, within the bound.
A program may use at most 128 MiB of HBM per device.

v0:
```python
import functools
import math

import jax
import jax.numpy as jnp
import ml_dtypes
import numpy as np
from jax import lax
from jax.experimental import pallas as pl
from jax.experimental.pallas import tpu as pltpu
from jax.sharding import PartitionSpec as P

F = 512
FLOW = 64
LAGS = 512
BLOCK = 256
MESH = pl.DeviceIdType.MESH


def make_tables(ticks):
    rate = FLOW + np.arange(F, dtype=np.int64)
    angles = (np.arange(ticks)[:, None] * rate[None, :] % ticks) * (2.0 * math.pi / ticks)
    forward = np.concatenate([np.cos(angles), -np.sin(angles)], 1) / math.sqrt(ticks)
    shifts = np.arange(LAGS, dtype=np.int64) - LAGS // 2
    turning = (rate[:, None] * shifts[None, :] % ticks) * (2.0 * math.pi / ticks)
    lag = np.concatenate([np.cos(turning), -np.sin(turning)], 0) / math.sqrt(F)
    short = lambda x: x.astype(np.float32).astype(ml_dtypes.bfloat16)
    return short(forward), short(lag)


def dot(a, b):
    return jnp.dot(a, b, preferred_element_type=jnp.float32)


def one_hot(condition):
    return jnp.where(condition, 1.0, 0.0).astype(jnp.bfloat16)


def iota(shape, axis):
    return lax.broadcasted_iota(jnp.int32, shape, axis)


def down(row, width):
    pairs = row.shape[1]
    column = jnp.transpose(jnp.broadcast_to(row.astype(jnp.float32), (128, pairs)))
    return jnp.concatenate([column] * (width // 128), 1).astype(jnp.int32)


def kernel(
    regions, peers, cap, local,
    syn_ref, obs_ref, near_ref, far_ref, first_ref, second_ref, start_ref, length_ref,
    w_hbm, wt_hbm, lag_hbm, lagt_hbm,
    adj_ref, misfit_ref,
    w, wt, lag, lagt, far_in, sp, send, recv, gout, gin, own, pick, spread, sel_out, sel_in,
    inside, energy, grads,
    w_sem, table_sem, idx_send, idx_recv, send_sem, recv_sem, gsend_sem, grecv_sem,
):
    region, me = lax.axis_index("region"), lax.axis_index("dev")
    last = regions - 1
    sources = 2 * peers
    rows = sources * 16
    pairs = first_ref.shape[1]

    w_copies = [pltpu.make_async_copy(w_hbm.at[i], w.at[i], w_sem.at[i]) for i in range(4)]
    table_copies = [
        pltpu.make_async_copy(a, b, table_sem.at[i])
        for i, (a, b) in enumerate(((lag_hbm, lag), (lagt_hbm, lagt), (wt_hbm, wt)))
    ]
    for copy in w_copies + table_copies:
        copy.start()

    barrier = pltpu.get_barrier_semaphore()

    def greet(j, carry):
        @pl.when(j != me)
        def _():
            pl.semaphore_signal(barrier, inc=1, device_id=(region, j), device_id_type=MESH)

        @pl.when(region > 0)
        def _():
            pl.semaphore_signal(barrier, inc=1, device_id=(region - 1, j), device_id_type=MESH)

        @pl.when(region < last)
        def _():
            pl.semaphore_signal(barrier, inc=1, device_id=(region + 1, j), device_id_type=MESH)

        return carry

    lax.fori_loop(0, peers, greet, 0)
    below = jnp.where(region > 0, peers, 0)
    above = jnp.where(region < last, peers, 0)
    pl.semaphore_wait(barrier, peers - 1 + below + above)

    def idx_copy(target):
        return pltpu.make_async_remote_copy(
            src_ref=far_ref, dst_ref=far_in, send_sem=idx_send, recv_sem=idx_recv,
            device_id=(target, me), device_id_type=MESH,
        )

    @pl.when(region < last)
    def _():
        idx_copy(region + 1).start()

    @pl.when(region == 0)
    def _():
        far_in[...] = jnp.zeros_like(far_in)
        gin[:, peers:sources] = jnp.zeros((3, peers, 16, BLOCK), jnp.bfloat16)

    @pl.when(region == last)
    def _():
        recv[:, peers:sources] = jnp.zeros((3, peers, 16, F), jnp.bfloat16)

    for end, ref in enumerate((first_ref, second_ref)):
        slot = ref[...]
        base = (slot >> 2) * 16 + (slot & 3)
        column = down(base, rows)
        lanes = iota((pairs, rows), 1)
        ups = iota((rows, pairs), 0)
        for o in range(4):
            at = (end * 4 + o) * pairs
            pick[at : at + pairs, :] = one_hot(lanes == column + 4 * o)
            spread[:, at : at + pairs] = one_hot(ups == base + 4 * o)
    position = iota((pairs, LAGS), 1)
    begin = down(start_ref[...], LAGS)
    stop = down(start_ref[...] + length_ref[...], LAGS)
    inside[...] = jnp.where((position >= begin) & (position < stop), 1.0, 0.0)
    energy[...] = jnp.zeros_like(energy)

    x = jnp.concatenate(
        [syn_ref[...].reshape(3 * local, -1), obs_ref[...].reshape(3 * local, -1)], 0
    )
    for i in range(4):
        w_copies[i].wait()
        part, half = i // 2, i % 2
        y = dot(x, w[i]).astype(jnp.bfloat16)
        for k in range(2):
            for c in range(3):
                at = part * 32 + k * 16
                sp[c, at : at + 16, half * BLOCK : (half + 1) * BLOCK] = y[
                    k * 48 + c * 16 : k * 48 + c * 16 + 16
                ]

    @pl.when(region > 0)
    def _():
        idx_copy(region).wait_recv()

    near_owner = jnp.where(iota((peers, rows), 1) // 16 == iota((peers, rows), 0), 1.0, 0.0)
    far_owner = jnp.where(
        iota((peers, rows), 1) // 16 == iota((peers, rows), 0) + peers, 1.0, 0.0
    )
    wide = dot(near_ref[...].astype(jnp.float32), near_owner)
    wide += dot(far_in[...].astype(jnp.float32), far_owner)
    wide = jnp.where(iota((cap, rows), 1) % 4 == iota((cap, rows), 0), wide, 0.0)
    asked_row = jnp.broadcast_to(jnp.sum(wide, 0, keepdims=True), (128, rows))
    asked_col = jnp.transpose(asked_row)
    asked_row = asked_row[:64].astype(jnp.int32)
    row = iota((rows, 64), 0)
    column = (row // 4 % 2) * 32 + (row // 8 % 2) * 16 + asked_col[:, :64].astype(jnp.int32)
    sel_out[...] = one_hot(column == iota((rows, 64), 1))
    up = iota((64, rows), 0)
    sel_in[...] = one_hot((asked_row == up % 16) & (iota((64, rows), 1) // 4 % 4 == up // 16))

    def spectra_copy(c, to, src, dst, target):
        return pltpu.make_async_remote_copy(
            src_ref=send.at[c, src], dst_ref=recv.at[c, dst],
            send_sem=send_sem.at[c, src], recv_sem=recv_sem.at[c, dst],
            device_id=(to, target), device_id_type=MESH,
        )

    def grad_copy(c, to, src, dst, target):
        return pltpu.make_async_remote_copy(
            src_ref=gout.at[c, src], dst_ref=gin.at[c, dst],
            send_sem=gsend_sem.at[c, src], recv_sem=grecv_sem.at[c, dst],
            device_id=(to, target), device_id_type=MESH,
        )

    def exchange(c, carry):
        block = dot(sel_out[...], sp[c]).astype(jnp.bfloat16)
        send[c] = block.reshape(sources, 16, F)
        recv[c, me] = send[c, me]

        def go(i, carry):
            j = (me + 1 + i) % peers

            @pl.when(j != me)
            def _():
                spectra_copy(c, region, j, me, j).start()

            @pl.when(region > 0)
            def _():
                spectra_copy(c, region - 1, peers + j, peers + me, j).start()

            return carry

        return lax.fori_loop(0, peers, go, carry)

    lax.fori_loop(0, 3, exchange, 0)

    table_copies[0].wait()
    table_copies[1].wait()

    def work(c, carry):
        def arrive(j, carry):
            @pl.when(j != me)
            def _():
                spectra_copy(c, region, j, j, j).wait_recv()

            @pl.when(region < last)
            def _():
                spectra_copy(c, region, peers + j, peers + j, j).wait_recv()

            return carry

        lax.fori_loop(0, peers, arrive, 0)
        fetched = recv[c].reshape(rows, F)
        got = lambda end, o: dot(pick[(end * 4 + o) * pairs : (end * 4 + o + 1) * pairs], fetched)
        ar, ai, br, bi = got(0, 0), got(0, 1), got(1, 0), got(1, 1)
        ur, ui, vr, vi = got(0, 2), got(0, 3), got(1, 2), got(1, 3)
        change_re = ((ar * br + ai * bi) - (ur * vr + ui * vi)).astype(jnp.bfloat16)
        change_im = ((ai * br - ar * bi) - (ui * vr - ur * vi)).astype(jnp.bfloat16)
        shifted = dot(change_re, lag[:F]) + dot(change_im, lag[F:])
        residual = jnp.where(inside[...] > 0.5, shifted, 0.0)
        energy[...] += residual * residual
        short = residual.astype(jnp.bfloat16)
        gr, gi = dot(short, lagt[:, :F]), dot(short, lagt[:, F:])
        ends = (
            (gr * br - gi * bi, gr * bi + gi * br),
            (gr * ar + gi * ai, gr * ai - gi * ar),
        )
        for end in range(2):
            for part in range(2):
                value = ends[end][part].astype(jnp.bfloat16)
                for half in range(2):
                    at = (end * 4 + half * 2 + part) * pairs
                    grads[at : at + pairs] = value[:, half * BLOCK : (half + 1) * BLOCK]
        total = dot(spread[...], grads[...]).astype(jnp.bfloat16)
        gout[c] = total.reshape(sources, 16, BLOCK)
        gin[c, me] = gout[c, me]

        def go(i, carry):
            j = (me + 1 + i) % peers

            @pl.when(j != me)
            def _():
                grad_copy(c, region, j, me, j).start()

            @pl.when(region < last)
            def _():
                grad_copy(c, region + 1, peers + j, peers + me, j).start()

            return carry

        return lax.fori_loop(0, peers, go, carry)

    lax.fori_loop(0, 3, work, 0)

    power = energy[:, :128]
    for i in range(1, LAGS // 128):
        power = power + energy[:, i * 128 : (i + 1) * 128]
    misfit_ref[...] = jnp.sum(jnp.transpose(power), 0, keepdims=True) / (2.0 * LAGS)

    def settle(c, carry):
        def arrive(j, carry):
            @pl.when(j != me)
            def _():
                grad_copy(c, region, j, j, j).wait_recv()

            @pl.when(region > 0)
            def _():
                grad_copy(c, region, peers + j, peers + j, j).wait_recv()

            return carry

        lax.fori_loop(0, peers, arrive, 0)
        total = dot(sel_in[...], gin[c].reshape(rows, BLOCK)).astype(jnp.bfloat16)
        for half in range(2):
            for part in range(2):
                o = half * 2 + part
                at = part * F + half * BLOCK
                own[c, :, at : at + BLOCK] = total[o * 16 : o * 16 + 16]
        return carry

    lax.fori_loop(0, 3, settle, 0)

    table_copies[2].wait()
    gathered = own[...].reshape(3 * local, 2 * F)
    width = wt.shape[2]

    def back(i, carry):
        at = pl.ds(pl.multiple_of(i * width, width), width)
        adj_ref[:, at] = dot(gathered, wt[i]).astype(jnp.bfloat16)
        return carry

    lax.fori_loop(0, wt.shape[0], back, 0)

    def sent(i, carry):
        c, j = i // peers, i % peers

        @pl.when(j != me)
        def _():
            spectra_copy(c, region, j, j, j).wait_send()
            grad_copy(c, region, j, j, j).wait_send()

        @pl.when(region > 0)
        def _():
            spectra_copy(c, region, peers + j, peers + j, j).wait_send()

        @pl.when(region < last)
        def _():
            grad_copy(c, region, peers + j, peers + j, j).wait_send()

        return carry

    lax.fori_loop(0, 3 * peers, sent, 0)

    @pl.when(region < last)
    def _():
        idx_copy(region).wait_send()


def on_device(
    regions, peers, synthetic, observed, nearby, far_rows, first, second, start, length
):
    local, _, ticks = synthetic.shape
    cap = nearby.shape[1]
    pairs = first.shape[0]
    forward, lag = make_tables(ticks)
    w = jnp.asarray(np.ascontiguousarray(forward.reshape(ticks, 4, BLOCK).transpose(1, 0, 2)))
    wt = jnp.asarray(
        np.ascontiguousarray(forward.T.reshape(2 * F, ticks // 512, 512).transpose(1, 0, 2))
    )
    lagt = jnp.asarray(np.ascontiguousarray(lag.T))
    lag = jnp.asarray(lag)
    sources = 2 * peers
    rows = sources * 16
    vmem = pl.BlockSpec(memory_space=pltpu.VMEM)
    hbm = pl.BlockSpec(memory_space=pl.ANY)
    b16, f32 = jnp.bfloat16, jnp.float32
    adj, misfit = pl.pallas_call(
        functools.partial(kernel, regions, peers, cap, local),
        out_shape=(
            jax.ShapeDtypeStruct((3 * local, ticks), b16),
            jax.ShapeDtypeStruct((1, pairs), f32),
        ),
        in_specs=[vmem] * 8 + [hbm] * 4,
        out_specs=(vmem, vmem),
        scratch_shapes=[
            pltpu.VMEM(w.shape, b16),
            pltpu.VMEM(wt.shape, b16),
            pltpu.VMEM(lag.shape, b16),
            pltpu.VMEM(lagt.shape, b16),
            pltpu.VMEM((cap, peers), jnp.int32),
            pltpu.VMEM((3, 4 * local, F), b16),
            pltpu.VMEM((3, sources, 16, F), b16),
            pltpu.VMEM((3, sources, 16, F), b16),
            pltpu.VMEM((3, sources, 16, BLOCK), b16),
            pltpu.VMEM((3, sources, 16, BLOCK), b16),
            pltpu.VMEM((3, local, 2 * F), b16),
            pltpu.VMEM((8 * pairs, rows), b16),
            pltpu.VMEM((rows, 8 * pairs), b16),
            pltpu.VMEM((rows, 64), b16),
            pltpu.VMEM((64, rows), b16),
            pltpu.VMEM((pairs, LAGS), f32),
            pltpu.VMEM((pairs, LAGS), f32),
            pltpu.VMEM((8 * pairs, BLOCK), b16),
            pltpu.SemaphoreType.DMA((4,)),
            pltpu.SemaphoreType.DMA((3,)),
            pltpu.SemaphoreType.DMA,
            pltpu.SemaphoreType.DMA,
            pltpu.SemaphoreType.DMA((3, sources)),
            pltpu.SemaphoreType.DMA((3, sources)),
            pltpu.SemaphoreType.DMA((3, sources)),
            pltpu.SemaphoreType.DMA((3, sources)),
        ],
        compiler_params=pltpu.CompilerParams(
            collective_id=0, has_side_effects=True, vmem_limit_bytes=60 * 1024 * 1024
        ),
    )(
        synthetic.transpose(1, 0, 2), observed.transpose(1, 0, 2), nearby.T, far_rows.T,
        first.reshape(1, pairs), second.reshape(1, pairs),
        start.reshape(1, pairs), length.reshape(1, pairs), w, wt, lag, lagt,
    )
    return adj.reshape(3, local, ticks).transpose(1, 0, 2), misfit.reshape(pairs)


def solution(mesh):
    placed = (P(("region", "dev"), None, None),) * 2 + (P(("region", "dev"), None),) * 2
    placed += (P(("region", "dev")),) * 4
    return jax.shard_map(
        functools.partial(on_device, mesh.shape["region"], mesh.shape["dev"]),
        mesh=mesh,
        in_specs=placed,
        out_specs=(P(("region", "dev"), None, None), P(("region", "dev"))),
        check_vma=False,
    )
```

profile of v0, /device:TPU:1, one launch (start us, length us, event | category | flops | bytes accessed | tf_op | source)
XLA Modules:
  0.0 48.3 jit_solution(9923166980725036551)
XLA Ops:
  0.6 44.7 %shard_map.131 = (bf16[48,4096]{1,0:T(8,128)(2,1)}, f32[1,256]{1,0:T(1,128)}) custom-call(bf16[3,16,4096]{2,1,0:T(8,128)(2,1)} %bitcast.13, bf16[3,16,4096]{2,1,0:T(8,128)(2,1)} %bitcast.14, s32[4,8]{1,0:T(4,128)} %bitcast.15, s32[4,8]{1,0:T(4,128)} %bitcast.16, s32[1,256]{1,0:T(1,128)} %bitcast.17, s32[1,256]{1,0:T(1,128)} %bitcast.18, s32[1,256]{1,0:T(1,128)} %bitcast.19, ...), custom_call_target="tpu_custom_call" | custom-call | tf_op jit(solution)/shard_map/pallas_call | solution.py:339
  45.3 1.8 %copy.16 = bf16[16,3,4096]{2,0,1:T(8,128)(2,1)} copy(bf16[16,3,4096]{2,0,1:T(8,128)(2,1)} %bitcast.12) | data formatting | bytes 786432
  47.1 1.2 %copy.17 = f32[256]{0:T(256)} copy(f32[256]{0:T(256)} %bitcast.21) | data formatting | bytes 2048
where the time goes:
time: 48.4 us; the launch traced here: 48.3 us
  Pallas kernels  44.7 us (92%)
  local copies, waits for them, and re-layouts  2.96 us (6%)
  between operations  0.64 us (1%)
    pallas_call x1, Pallas kernels, on_device(): pl.pallas_call(functools.partial(kernel, regions, peers, cap, local), out...  44.7 us
    unnamed x2, local copies, waits for them, and re-layouts  2.96 us

commit v1 on v0

--- a/solution.py
+++ b/solution.py
@@ -109,6 +109,84 @@
     @pl.when(region == last)
     def _():
         recv[:, peers:sources] = jnp.zeros((3, peers, 16, F), jnp.bfloat16)
+
+    count = 6 * local
+    x = jnp.concatenate(
+        [syn_ref[...].reshape(3 * local, -1), obs_ref[...].reshape(3 * local, -1)], 0
+    ).astype(jnp.float32)
+    middle = x.shape[1] // 2
+    for half in range(2):
+        x0, x1 = x[:, :middle], x[:, middle:]
+        folded = x0 - x1 if half else x0 + x1
+        high = folded.astype(jnp.bfloat16)
+        low = (folded - high.astype(jnp.float32)).astype(jnp.bfloat16)
+        both = jnp.concatenate([high, low], 0)
+        for part in range(2):
+            w_copies[half * 2 + part].wait()
+            y = dot(both, w[half * 2 + part])
+            y = (y[:count] + y[count:]).astype(jnp.bfloat16)
+            for k in range(2):
+                for c in range(3):
+                    at = part * 32 + k * 16
+                    sp[c, at : at + 16, half * BLOCK : (half + 1) * BLOCK] = y[
+                        k * 48 + c * 16 : k * 48 + c * 16 + 16
+                    ]
+
+    @pl.when(region > 0)
+    def _():
+        idx_copy(region).wait_recv()
+
+    near_owner = jnp.where(iota((peers, rows), 1) // 16 == iota((peers, rows), 0), 1.0, 0.0)
+    far_owner = jnp.where(
+        iota((peers, rows), 1) // 16 == iota((peers, rows), 0) + peers, 1.0, 0.0
+    )
+    wide = dot(near_ref[...].astype(jnp.float32), near_owner)
+    wide += dot(far_in[...].astype(jnp.float32), far_owner)
+    wide = jnp.where(iota((cap, rows), 1) % 4 == iota((cap, rows), 0), wide, 0.0)
+    asked_row = jnp.broadcast_to(jnp.sum(wide, 0, keepdims=True), (128, rows))
+    asked_col = jnp.transpose(asked_row)
+    asked_row = asked_row[:64].astype(jnp.int32)
+    row = iota((rows, 64), 0)
+    column = (row // 4 % 2) * 32 + (row // 8 % 2) * 16 + asked_col[:, :64].astype(jnp.int32)
+    sel_out[...] = one_hot(column == iota((rows, 64), 1))
+    up = iota((64, rows), 0)
+    sel_in[...] = one_hot((asked_row == up % 16) & (iota((64, rows), 1) // 4 % 4 == up // 16))
+
+    def spectra_copy(c, to, src, dst, target):
+        return pltpu.make_async_remote_copy(
+            src_ref=send.at[c, src], dst_ref=recv.at[c, dst],
+            send_sem=send_sem.at[c, src], recv_sem=recv_sem.at[c, dst],
+            device_id=(to, target), device_id_type=MESH,
+        )
+
+    def grad_copy(c, to, src, dst, target):
+        return pltpu.make_async_remote_copy(
+            src_ref=gout.at[c, src], dst_ref=gin.at[c, dst],
+            send_sem=gsend_sem.at[c, src], recv_sem=grecv_sem.at[c, dst],
+            device_id=(to, target), device_id_type=MESH,
+        )
+
+    def exchange(c, carry):
+        block = dot(sel_out[...], sp[c]).astype(jnp.bfloat16)
+        send[c] = block.reshape(sources, 16, F)
+        recv[c, me] = send[c, me]
+
+        def go(i, carry):
+            j = (me + 1 + i) % peers
+
+            @pl.when(j != me)
+            def _():
+                spectra_copy(c, region, j, me, j).start()
+
+            @pl.when(region > 0)
+            def _():
+                spectra_copy(c, region - 1, peers + j, peers + me, j).start()
+
+            return carry
+
+        return lax.fori_loop(0, peers, go, carry)
+
+    lax.fori_loop(0, 3, exchange, 0)
 
     for end, ref in enumerate((first_ref, second_ref)):
         slot = ref[...]
@@ -125,76 +203,6 @@
     stop = down(start_ref[...] + length_ref[...], LAGS)
     inside[...] = jnp.where((position >= begin) & (position < stop), 1.0, 0.0)
     energy[...] = jnp.zeros_like(energy)
-
-    x = jnp.concatenate(
-        [syn_ref[...].reshape(3 * local, -1), obs_ref[...].reshape(3 * local, -1)], 0
-    )
-    for i in range(4):
-        w_copies[i].wait()
-        part, half = i // 2, i % 2
-        y = dot(x, w[i]).astype(jnp.bfloat16)
-        for k in range(2):
-            for c in range(3):
-                at = part * 32 + k * 16
-                sp[c, at : at + 16, half * BLOCK : (half + 1) * BLOCK] = y[
-                    k * 48 + c * 16 : k * 48 + c * 16 + 16
-                ]
-
-    @pl.when(region > 0)
-    def _():
-        idx_copy(region).wait_recv()
-
-    near_owner = jnp.where(iota((peers, rows), 1) // 16 == iota((peers, rows), 0), 1.0, 0.0)
-    far_owner = jnp.where(
-        iota((peers, rows), 1) // 16 == iota((peers, rows), 0) + peers, 1.0, 0.0
-    )
-    wide = dot(near_ref[...].astype(jnp.float32), near_owner)
-    wide += dot(far_in[...].astype(jnp.float32), far_owner)
-    wide = jnp.where(iota((cap, rows), 1) % 4 == iota((cap, rows), 0), wide, 0.0)
-    asked_row = jnp.broadcast_to(jnp.sum(wide, 0, keepdims=True), (128, rows))
-    asked_col = jnp.transpose(asked_row)
-    asked_row = asked_row[:64].astype(jnp.int32)
-    row = iota((rows, 64), 0)
-    column = (row // 4 % 2) * 32 + (row // 8 % 2) * 16 + asked_col[:, :64].astype(jnp.int32)
-    sel_out[...] = one_hot(column == iota((rows, 64), 1))
-    up = iota((64, rows), 0)
-    sel_in[...] = one_hot((asked_row == up % 16) & (iota((64, rows), 1) // 4 % 4 == up // 16))
-
-    def spectra_copy(c, to, src, dst, target):
-        return pltpu.make_async_remote_copy(
-            src_ref=send.at[c, src], dst_ref=recv.at[c, dst],
-            send_sem=send_sem.at[c, src], recv_sem=recv_sem.at[c, dst],
-            device_id=(to, target), device_id_type=MESH,
-        )
-
-    def grad_copy(c, to, src, dst, target):
-        return pltpu.make_async_remote_copy(
-            src_ref=gout.at[c, src], dst_ref=gin.at[c, dst],
-            send_sem=gsend_sem.at[c, src], recv_sem=grecv_sem.at[c, dst],
-            device_id=(to, target), device_id_type=MESH,
-        )
-
-    def exchange(c, carry):
-        block = dot(sel_out[...], sp[c]).astype(jnp.bfloat16)
-        send[c] = block.reshape(sources, 16, F)
-        recv[c, me] = send[c, me]
-
-        def go(i, carry):
-            j = (me + 1 + i) % peers
-
-            @pl.when(j != me)
-            def _():
-                spectra_copy(c, region, j, me, j).start()
-
-            @pl.when(region > 0)
-            def _():
-                spectra_copy(c, region - 1, peers + j, peers + me, j).start()
-
-            return carry
-
-        return lax.fori_loop(0, peers, go, carry)
-
-    lax.fori_loop(0, 3, exchange, 0)
 
     table_copies[0].wait()
     table_copies[1].wait()
@@ -276,19 +284,21 @@
         for half in range(2):
             for part in range(2):
                 o = half * 2 + part
-                at = part * F + half * BLOCK
-                own[c, :, at : at + BLOCK] = total[o * 16 : o * 16 + 16]
+                own[half, c, :, part * BLOCK : (part + 1) * BLOCK] = total[o * 16 : o * 16 + 16]
         return carry
 
     lax.fori_loop(0, 3, settle, 0)
 
     table_copies[2].wait()
-    gathered = own[...].reshape(3 * local, 2 * F)
-    width = wt.shape[2]
+    even = own[0].reshape(3 * local, F)
+    odd = own[1].reshape(3 * local, F)
+    width = wt.shape[3]
 
     def back(i, carry):
-        at = pl.ds(pl.multiple_of(i * width, width), width)
-        adj_ref[:, at] = dot(gathered, wt[i]).astype(jnp.bfloat16)
+        at = pl.multiple_of(i * width, width)
+        plain, signed = dot(even, wt[i, 0]), dot(odd, wt[i, 1])
+        adj_ref[:, pl.ds(at, width)] = (plain + signed).astype(jnp.bfloat16)
+        adj_ref[:, pl.ds(at + middle, width)] = (plain - signed).astype(jnp.bfloat16)
         return carry
 
     lax.fori_loop(0, wt.shape[0], back, 0)
@@ -325,12 +335,14 @@
     cap = nearby.shape[1]
     pairs = first.shape[0]
     forward, lag = make_tables(ticks)
-    w = jnp.asarray(np.ascontiguousarray(forward.reshape(ticks, 4, BLOCK).transpose(1, 0, 2)))
-    wt = jnp.asarray(
-        np.ascontiguousarray(forward.T.reshape(2 * F, ticks // 512, 512).transpose(1, 0, 2))
-    )
-    lagt = jnp.asarray(np.ascontiguousarray(lag.T))
-    lag = jnp.asarray(lag)
+    middle, width = ticks // 2, 512
+    forward = forward[:middle].reshape(middle, 2, F // 2, 2).transpose(3, 1, 2, 0)
+    lag = lag.reshape(2, F // 2, 2, LAGS).transpose(0, 2, 1, 3).reshape(2 * F, LAGS)
+    plain = lambda a: jnp.asarray(np.ascontiguousarray(a))
+    w = plain(forward.reshape(4, BLOCK, middle).transpose(0, 2, 1))
+    wt = plain(forward.reshape(2, F, middle // width, width).transpose(2, 0, 1, 3))
+    lagt = plain(lag.T)
+    lag = plain(lag)
     sources = 2 * peers
     rows = sources * 16
     vmem = pl.BlockSpec(memory_space=pltpu.VMEM)
@@ -355,7 +367,7 @@
             pltpu.VMEM((3, sources, 16, F), b16),
             pltpu.VMEM((3, sources, 16, BLOCK), b16),
             pltpu.VMEM((3, sources, 16, BLOCK), b16),
-            pltpu.VMEM((3, local, 2 * F), b16),
+            pltpu.VMEM((2, 3, local, F), b16),
             pltpu.VMEM((8 * pairs, rows), b16),
             pltpu.VMEM((rows, 8 * pairs), b16),
             pltpu.VMEM((rows, 64), b16),

time: 48.4 us -> 46.3 us (0.957)
  Pallas kernels: 44.7 us -> 42.5 us
    pallas_call x1, Pallas kernels: 44.7 us -> 42.5 us  [on_device(): pl.pallas_call(functools.partial(kernel, regions, peers, cap, local), out...]
where the time goes in v1:
time: 46.3 us; the launch traced here: 46.1 us
  Pallas kernels  42.5 us (92%)
  local copies, waits for them, and re-layouts  2.96 us (6%)
  between operations  0.64 us (1%)
    pallas_call x1, Pallas kernels, on_device(): pl.pallas_call(functools.partial(kernel, regions, peers, cap, local), out...  42.5 us
    unnamed x2, local copies, waits for them, and re-layouts  2.96 us

profile of v1, /device:TPU:1, one launch (start us, length us, event | category | flops | bytes accessed | tf_op | source)
XLA Modules:
  0.0 46.1 jit_solution(4597956995336627101)
XLA Ops:
  0.6 42.5 %shard_map.131 = (bf16[48,4096]{1,0:T(8,128)(2,1)}, f32[1,256]{1,0:T(1,128)}) custom-call(bf16[3,16,4096]{2,1,0:T(8,128)(2,1)} %bitcast.12, bf16[3,16,4096]{2,1,0:T(8,128)(2,1)} %bitcast.13, s32[4,8]{1,0:T(4,128)} %bitcast.15, s32[4,8]{1,0:T(4,128)} %bitcast.16, s32[1,256]{1,0:T(1,128)} %bitcast.17, s32[1,256]{1,0:T(1,128)} %bitcast.18, s32[1,256]{1,0:T(1,128)} %bitcast.19, ...), custom_call_target="tpu_custom_call" | custom-call | tf_op jit(solution)/shard_map/pallas_call | solution.py:351
  43.2 1.8 %copy.16 = bf16[16,3,4096]{2,0,1:T(8,128)(2,1)} copy(bf16[16,3,4096]{2,0,1:T(8,128)(2,1)} %bitcast.14) | data formatting | bytes 786432
  44.9 1.2 %copy.17 = f32[256]{0:T(256)} copy(f32[256]{0:T(256)} %bitcast.21) | data formatting | bytes 2048

commit v2 on v1

--- a/solution.py
+++ b/solution.py
@@ -186,7 +186,7 @@
 
         return lax.fori_loop(0, peers, go, carry)
 
-    lax.fori_loop(0, 3, exchange, 0)
+    lax.fori_loop(0, 2, exchange, 0)
 
     for end, ref in enumerate((first_ref, second_ref)):
         slot = ref[...]
@@ -220,6 +220,11 @@
             return carry
 
         lax.fori_loop(0, peers, arrive, 0)
+
+        @pl.when(c == 0)
+        def _():
+            exchange(2, 0)
+
         fetched = recv[c].reshape(rows, F)
         got = lambda end, o: dot(pick[(end * 4 + o) * pairs : (end * 4 + o + 1) * pairs], fetched)
         ar, ai, br, bi = got(0, 0), got(0, 1), got(1, 0), got(1, 1)

time: 46.3 us -> 46.3 us (level)
  no operation moved by 1% of the time
where the time goes in v2:
time: 46.3 us; the launch traced here: 46.1 us
  Pallas kernels  42.5 us (92%)
  local copies, waits for them, and re-layouts  2.96 us (6%)
  between operations  0.64 us (1%)
    pallas_call x1, Pallas kernels, on_device(): pl.pallas_call(functools.partial(kernel, regions, peers, cap, local), out...  42.5 us
    unnamed x2, local copies, waits for them, and re-layouts  2.96 us

profile of v2, /device:TPU:1, one launch (start us, length us, event | category | flops | bytes accessed | tf_op | source)
XLA Modules:
  0.0 46.1 jit_solution(5153735017129333768)
XLA Ops:
  0.6 42.5 %shard_map.131 = (bf16[48,4096]{1,0:T(8,128)(2,1)}, f32[1,256]{1,0:T(1,128)}) custom-call(bf16[3,16,4096]{2,1,0:T(8,128)(2,1)} %bitcast.12, bf16[3,16,4096]{2,1,0:T(8,128)(2,1)} %bitcast.13, s32[4,8]{1,0:T(4,128)} %bitcast.15, s32[4,8]{1,0:T(4,128)} %bitcast.16, s32[1,256]{1,0:T(1,128)} %bitcast.17, s32[1,256]{1,0:T(1,128)} %bitcast.18, s32[1,256]{1,0:T(1,128)} %bitcast.19, ...), custom_call_target="tpu_custom_call" | custom-call | tf_op jit(solution)/shard_map/pallas_call | solution.py:356
  43.2 1.8 %copy.16 = bf16[16,3,4096]{2,0,1:T(8,128)(2,1)} copy(bf16[16,3,4096]{2,0,1:T(8,128)(2,1)} %bitcast.14) | data formatting | bytes 786432
  44.9 1.2 %copy.17 = f32[256]{0:T(256)} copy(f32[256]{0:T(256)} %bitcast.21) | data formatting | bytes 2048

commit v3 on v1

--- a/solution.py
+++ b/solution.py
@@ -52,7 +52,7 @@
     w_hbm, wt_hbm, lag_hbm, lagt_hbm,
     adj_ref, misfit_ref,
     w, wt, lag, lagt, far_in, sp, send, recv, gout, gin, own, pick, spread, sel_out, sel_in,
-    inside, energy, grads,
+    inside, energy, grads, got, change, slope,
     w_sem, table_sem, idx_send, idx_recv, send_sem, recv_sem, gsend_sem, grecv_sem,
 ):
     region, me = lax.axis_index("region"), lax.axis_index("dev")
@@ -221,26 +221,46 @@
 
         lax.fori_loop(0, peers, arrive, 0)
         fetched = recv[c].reshape(rows, F)
-        got = lambda end, o: dot(pick[(end * 4 + o) * pairs : (end * 4 + o + 1) * pairs], fetched)
-        ar, ai, br, bi = got(0, 0), got(0, 1), got(1, 0), got(1, 1)
-        ur, ui, vr, vi = got(0, 2), got(0, 3), got(1, 2), got(1, 3)
-        change_re = ((ar * br + ai * bi) - (ur * vr + ui * vi)).astype(jnp.bfloat16)
-        change_im = ((ai * br - ar * bi) - (ui * vr - ur * vi)).astype(jnp.bfloat16)
-        shifted = dot(change_re, lag[:F]) + dot(change_im, lag[F:])
-        residual = jnp.where(inside[...] > 0.5, shifted, 0.0)
+        for v in range(8):
+            got[v] = dot(pick[v * pairs : (v + 1) * pairs], fetched).astype(jnp.bfloat16)
+        halves = [pl.ds(half * BLOCK, BLOCK) for half in range(2)]
+        imaginary = [pl.ds(F + half * BLOCK, BLOCK) for half in range(2)]
+
+        def cross(i, carry):
+            at = pl.ds(pl.multiple_of(i * 16, 16), 16)
+            for half in range(2):
+                ar, ai, ur, ui, br, bi, vr, vi = [
+                    got[v, at, halves[half]].astype(jnp.float32) for v in range(8)
+                ]
+                change_re = (ar * br + ai * bi) - (ur * vr + ui * vi)
+                change_im = (ai * br - ar * bi) - (ui * vr - ur * vi)
+                change[at, halves[half]] = change_re.astype(jnp.bfloat16)
+                change[at, imaginary[half]] = change_im.astype(jnp.bfloat16)
+            return carry
+
+        lax.fori_loop(0, pairs // 16, cross, 0, unroll=2)
+        shifted = dot(change[...], lag[...])
+        residual = shifted * inside[...]
         energy[...] += residual * residual
-        short = residual.astype(jnp.bfloat16)
-        gr, gi = dot(short, lagt[:, :F]), dot(short, lagt[:, F:])
-        ends = (
-            (gr * br - gi * bi, gr * bi + gi * br),
-            (gr * ar + gi * ai, gr * ai - gi * ar),
-        )
-        for end in range(2):
-            for part in range(2):
-                value = ends[end][part].astype(jnp.bfloat16)
-                for half in range(2):
-                    at = (end * 4 + half * 2 + part) * pairs
-                    grads[at : at + pairs] = value[:, half * BLOCK : (half + 1) * BLOCK]
+        slope[...] = dot(residual.astype(jnp.bfloat16), lagt[...])
+
+        def chain(i, carry):
+            at = pl.ds(pl.multiple_of(i * 16, 16), 16)
+            for half in range(2):
+                gr, gi = slope[at, halves[half]], slope[at, imaginary[half]]
+                ar, ai, br, bi = [
+                    got[v, at, halves[half]].astype(jnp.float32) for v in (0, 1, 4, 5)
+                ]
+                values = (
+                    gr * br - gi * bi, gr * bi + gi * br, gr * ar + gi * ai, gr * ai - gi * ar
+                )
+                for j in range(4):
+                    start = (j // 2 * 4 + half * 2 + j % 2) * pairs
+                    rows_at = pl.ds(pl.multiple_of(start + i * 16, 16), 16)
+                    grads[rows_at] = values[j].astype(jnp.bfloat16)
+            return carry
+
+        lax.fori_loop(0, pairs // 16, chain, 0, unroll=2)
         total = dot(spread[...], grads[...]).astype(jnp.bfloat16)
         gout[c] = total.reshape(sources, 16, BLOCK)
         gin[c, me] = gout[c, me]
@@ -375,6 +395,9 @@
             pltpu.VMEM((pairs, LAGS), f32),
             pltpu.VMEM((pairs, LAGS), f32),
             pltpu.VMEM((8 * pairs, BLOCK), b16),
+            pltpu.VMEM((8, pairs, F), b16),
+            pltpu.VMEM((pairs, 2 * F), b16),
+            pltpu.VMEM((pairs, 2 * F), f32),
             pltpu.SemaphoreType.DMA((4,)),
             pltpu.SemaphoreType.DMA((3,)),
             pltpu.SemaphoreType.DMA,

time: 46.3 us -> 46.6 us (level)
  no operation moved by 1% of the time
where the time goes in v3:
time: 46.6 us; the launch traced here: 46.4 us
  Pallas kernels  42.8 us (92%)
  local copies, waits for them, and re-layouts  2.96 us (6%)
  between operations  0.64 us (1%)
    pallas_call x1, Pallas kernels, on_device(): pl.pallas_call(functools.partial(kernel, regions, peers, cap, local), out...  42.8 us
    unnamed x2, local copies, waits for them, and re-layouts  2.96 us

profile of v3, /device:TPU:1, one launch (start us, length us, event | category | flops | bytes accessed | tf_op | source)
XLA Modules:
  0.0 46.4 jit_solution(13376079459701503510)
XLA Ops:
  0.6 42.8 %shard_map.131 = (bf16[48,4096]{1,0:T(8,128)(2,1)}, f32[1,256]{1,0:T(1,128)}) custom-call(bf16[3,16,4096]{2,1,0:T(8,128)(2,1)} %bitcast.12, bf16[3,16,4096]{2,1,0:T(8,128)(2,1)} %bitcast.13, s32[4,8]{1,0:T(4,128)} %bitcast.15, s32[4,8]{1,0:T(4,128)} %bitcast.16, s32[1,256]{1,0:T(1,128)} %bitcast.17, s32[1,256]{1,0:T(1,128)} %bitcast.18, s32[1,256]{1,0:T(1,128)} %bitcast.19, ...), custom_call_target="tpu_custom_call" | custom-call | tf_op jit(solution)/shard_map/pallas_call | solution.py:371
  43.5 1.8 %copy.16 = bf16[16,3,4096]{2,0,1:T(8,128)(2,1)} copy(bf16[16,3,4096]{2,0,1:T(8,128)(2,1)} %bitcast.14) | data formatting | bytes 786432
  45.2 1.2 %copy.17 = f32[256]{0:T(256)} copy(f32[256]{0:T(256)} %bitcast.21) | data formatting | bytes 2048

commit v4 on v1

--- a/solution.py
+++ b/solution.py
@@ -115,7 +115,7 @@
         [syn_ref[...].reshape(3 * local, -1), obs_ref[...].reshape(3 * local, -1)], 0
     ).astype(jnp.float32)
     middle = x.shape[1] // 2
-    for half in range(2):
+    def transform(half):
         x0, x1 = x[:, :middle], x[:, middle:]
         folded = x0 - x1 if half else x0 + x1
         high = folded.astype(jnp.bfloat16)
@@ -132,6 +132,8 @@
                         k * 48 + c * 16 : k * 48 + c * 16 + 16
                     ]
 
+    transform(0)
+
     @pl.when(region > 0)
     def _():
         idx_copy(region).wait_recv()
@@ -152,10 +154,15 @@
     up = iota((64, rows), 0)
     sel_in[...] = one_hot((asked_row == up % 16) & (iota((64, rows), 1) // 4 % 4 == up // 16))
 
-    def spectra_copy(c, to, src, dst, target):
+    def spectra_copy(group, to, src, dst, target):
+        if isinstance(group, int) and group < 2:
+            columns = pl.ds(group * BLOCK, BLOCK)
+            source, landing = send.at[0, src, :, columns], recv.at[0, dst, :, columns]
+        else:
+            source, landing = send.at[group - 1, src], recv.at[group - 1, dst]
         return pltpu.make_async_remote_copy(
-            src_ref=send.at[c, src], dst_ref=recv.at[c, dst],
-            send_sem=send_sem.at[c, src], recv_sem=recv_sem.at[c, dst],
+            src_ref=source, dst_ref=landing,
+            send_sem=send_sem.at[group, src], recv_sem=recv_sem.at[group, dst],
             device_id=(to, target), device_id_type=MESH,
         )
 
@@ -166,27 +173,32 @@
             device_id=(to, target), device_id_type=MESH,
         )
 
-    def exchange(c, carry):
-        block = dot(sel_out[...], sp[c]).astype(jnp.bfloat16)
-        send[c] = block.reshape(sources, 16, F)
-        recv[c, me] = send[c, me]
+    def exchange(group):
+        c = max(group - 1, 0)
+        columns = pl.ds(group * BLOCK, BLOCK) if group < 2 else pl.ds(0, F)
+        block = dot(sel_out[...], sp[c, :, columns]).astype(jnp.bfloat16)
+        send[c, :, :, columns] = block.reshape(sources, 16, -1)
+        recv[c, me, :, columns] = send[c, me, :, columns]
 
         def go(i, carry):
             j = (me + 1 + i) % peers
 
             @pl.when(j != me)
             def _():
-                spectra_copy(c, region, j, me, j).start()
+                spectra_copy(group, region, j, me, j).start()
 
             @pl.when(region > 0)
             def _():
-                spectra_copy(c, region - 1, peers + j, peers + me, j).start()
+                spectra_copy(group, region - 1, peers + j, peers + me, j).start()
 
             return carry
 
-        return lax.fori_loop(0, peers, go, carry)
-
-    lax.fori_loop(0, 3, exchange, 0)
+        lax.fori_loop(0, peers, go, 0)
+
+    exchange(0)
+    transform(1)
+    for group in range(1, 4):
+        exchange(group)
 
     for end, ref in enumerate((first_ref, second_ref)):
         slot = ref[...]
@@ -209,13 +221,23 @@
 
     def work(c, carry):
         def arrive(j, carry):
-            @pl.when(j != me)
-            def _():
-                spectra_copy(c, region, j, j, j).wait_recv()
-
-            @pl.when(region < last)
-            def _():
-                spectra_copy(c, region, peers + j, peers + j, j).wait_recv()
+            def take(group):
+                @pl.when(j != me)
+                def _():
+                    spectra_copy(group, region, j, j, j).wait_recv()
+
+                @pl.when(region < last)
+                def _():
+                    spectra_copy(group, region, peers + j, peers + j, j).wait_recv()
+
+            @pl.when(c == 0)
+            def _():
+                take(0)
+                take(1)
+
+            @pl.when(c > 0)
+            def _():
+                take(c + 1)
 
             return carry
 
@@ -303,25 +325,28 @@
 
     lax.fori_loop(0, wt.shape[0], back, 0)
 
-    def sent(i, carry):
-        c, j = i // peers, i % peers
-
-        @pl.when(j != me)
-        def _():
-            spectra_copy(c, region, j, j, j).wait_send()
-            grad_copy(c, region, j, j, j).wait_send()
-
-        @pl.when(region > 0)
-        def _():
-            spectra_copy(c, region, peers + j, peers + j, j).wait_send()
-
-        @pl.when(region < last)
-        def _():
-            grad_copy(c, region, peers + j, peers + j, j).wait_send()
+    def sent(j, carry):
+        for c in range(3):
+            @pl.when(j != me)
+            def _():
+                grad_copy(c, region, j, j, j).wait_send()
+
+            @pl.when(region < last)
+            def _():
+                grad_copy(c, region, peers + j, peers + j, j).wait_send()
+
+        for group in range(4):
+            @pl.when(j != me)
+            def _():
+                spectra_copy(group, region, j, j, j).wait_send()
+
+            @pl.when(region > 0)
+            def _():
+                spectra_copy(group, region, peers + j, peers + j, j).wait_send()
 
         return carry
 
-    lax.fori_loop(0, 3 * peers, sent, 0)
+    lax.fori_loop(0, peers, sent, 0)
 
     @pl.when(region < last)
     def _():
@@ -379,8 +404,8 @@
             pltpu.SemaphoreType.DMA((3,)),
             pltpu.SemaphoreType.DMA,
             pltpu.SemaphoreType.DMA,
-            pltpu.SemaphoreType.DMA((3, sources)),
-            pltpu.SemaphoreType.DMA((3, sources)),
+            pltpu.SemaphoreType.DMA((4, sources)),
+            pltpu.SemaphoreType.DMA((4, sources)),
             pltpu.SemaphoreType.DMA((3, sources)),
             pltpu.SemaphoreType.DMA((3, sources)),
         ],

time: 46.3 us -> 46 us (level)
  no operation moved by 1% of the time
where the time goes in v4:
time: 46 us; the launch traced here: 45.8 us
  Pallas kernels  42.2 us (92%)
  local copies, waits for them, and re-layouts  2.96 us (6%)
  between operations  0.64 us (1%)
    pallas_call x1, Pallas kernels, on_device(): pl.pallas_call(functools.partial(kernel, regions, peers, cap, local), out...  42.2 us
    unnamed x2, local copies, waits for them, and re-layouts  2.96 us

profile of v4, /device:TPU:1, one launch (start us, length us, event | category | flops | bytes accessed | tf_op | source)
XLA Modules:
  0.0 45.8 jit_solution(13977255310530853175)
XLA Ops:
  0.6 42.2 %shard_map.131 = (bf16[48,4096]{1,0:T(8,128)(2,1)}, f32[1,256]{1,0:T(1,128)}) custom-call(bf16[3,16,4096]{2,1,0:T(8,128)(2,1)} %bitcast.12, bf16[3,16,4096]{2,1,0:T(8,128)(2,1)} %bitcast.13, s32[4,8]{1,0:T(4,128)} %bitcast.15, s32[4,8]{1,0:T(4,128)} %bitcast.16, s32[1,256]{1,0:T(1,128)} %bitcast.17, s32[1,256]{1,0:T(1,128)} %bitcast.18, s32[1,256]{1,0:T(1,128)} %bitcast.19, ...), custom_call_target="tpu_custom_call" | custom-call | tf_op jit(solution)/shard_map/pallas_call | solution.py:376
  42.9 1.8 %copy.16 = bf16[16,3,4096]{2,0,1:T(8,128)(2,1)} copy(bf16[16,3,4096]{2,0,1:T(8,128)(2,1)} %bitcast.14) | data formatting | bytes 786432
  44.7 1.2 %copy.17 = f32[256]{0:T(256)} copy(f32[256]{0:T(256)} %bitcast.21) | data formatting | bytes 2048

commit v5 on v1

--- a/solution.py
+++ b/solution.py
@@ -172,7 +172,7 @@
         recv[c, me] = send[c, me]
 
         def go(i, carry):
-            j = (me + 1 + i) % peers
+            j = (me + peers // 2 + i) % peers
 
             @pl.when(j != me)
             def _():
@@ -246,7 +246,7 @@
         gin[c, me] = gout[c, me]
 
         def go(i, carry):
-            j = (me + 1 + i) % peers
+            j = (me + peers // 2 + i) % peers
 
             @pl.when(j != me)
             def _():

time: 46.3 us -> 46.1 us (level)
  no operation moved by 1% of the time
where the time goes in v5:
time: 46.1 us; the launch traced here: 45.9 us
  Pallas kernels  42.3 us (92%)
  local copies, waits for them, and re-layouts  2.96 us (6%)
  between operations  0.64 us (1%)
    pallas_call x1, Pallas kernels, on_device(): pl.pallas_call(functools.partial(kernel, regions, peers, cap, local), out...  42.3 us
    unnamed x2, local copies, waits for them, and re-layouts  2.96 us

profile of v5, /device:TPU:1, one launch (start us, length us, event | category | flops | bytes accessed | tf_op | source)
XLA Modules:
  0.0 45.9 jit_solution(9156222515780068175)
XLA Ops:
  0.6 42.3 %shard_map.131 = (bf16[48,4096]{1,0:T(8,128)(2,1)}, f32[1,256]{1,0:T(1,128)}) custom-call(bf16[3,16,4096]{2,1,0:T(8,128)(2,1)} %bitcast.12, bf16[3,16,4096]{2,1,0:T(8,128)(2,1)} %bitcast.13, s32[4,8]{1,0:T(4,128)} %bitcast.15, s32[4,8]{1,0:T(4,128)} %bitcast.16, s32[1,256]{1,0:T(1,128)} %bitcast.17, s32[1,256]{1,0:T(1,128)} %bitcast.18, s32[1,256]{1,0:T(1,128)} %bitcast.19, ...), custom_call_target="tpu_custom_call" | custom-call | tf_op jit(solution)/shard_map/pallas_call | solution.py:351
  43.0 1.8 %copy.16 = bf16[16,3,4096]{2,0,1:T(8,128)(2,1)} copy(bf16[16,3,4096]{2,0,1:T(8,128)(2,1)} %bitcast.14) | data formatting | bytes 786432
  44.7 1.2 %copy.17 = f32[256]{0:T(256)} copy(f32[256]{0:T(256)} %bitcast.21) | data formatting | bytes 2048
